TPU v7x, 512 devices: a whole 4x4x16 slice. The times are simulated.
512 devices in a mesh: brow: 16 (over z), bcol: 32 (over y, x, core).
Axes of the slice: x: 4, y: 4, z: 16, core: 2. Of those that a mesh axis runs over, the one named last changes fastest.
Arguments:
- ancestor_cov: bfloat16 [5632, 5632], P('brow', 'bcol'), may hold values from -1 to 4
- ancestor_pattern: int32 [22], replicated, may hold values 0 or 1
- parent_panel: bfloat16 [5632, 4096], P('brow'), may hold values from -0.5 to 0.5
- parent_inverse: bfloat16 [4096, 4096], P('brow', 'bcol'), may hold values from -1 to 4
- child_pattern: int32 [16], replicated, may hold values 0 or 1
- child_panel: bfloat16 [4096, 4096], P('brow', 'bcol'), may hold values from -0.3125 to 0.3125
- child_inverse: bfloat16 [4096, 4096], P('brow', 'bcol'), may hold values from -1 to 4
Outputs:
- ancestor_block: bfloat16 [5632, 4096], P('brow', 'bcol')
- parent_diag: bfloat16 [4096, 4096], P('brow', 'bcol')
- parent_child: bfloat16 [4096, 4096], P('brow', 'bcol')
- child_diag: bfloat16 [4096, 4096], P('brow', 'bcol')
All inputs are finite; a program needn't handle non-finite values.
Results may differ from a plain program's by a relative error of at most 0.006.
Values may be sent and summed in bfloat16 or wider, within the bound.
No kernel may reach another device: no remote copies, remote signals or barrier semaphores. Data moves between devices by JAX's collectives and lax.ppermute only.
A program may use at most 64 MiB of HBM per device.

v0:
```python
import jax
import jax.numpy as jnp
from jax import lax
from jax.sharding import PartitionSpec as P


def block_keep(pattern, first_row, count, total_rows):
    block_rows = total_rows // pattern.shape[0]
    row_ids = first_row + lax.iota(jnp.int32, count)
    block_ids = lax.iota(jnp.int32, pattern.shape[0])
    matches = row_ids[:, None] // block_rows == block_ids[None, :]
    return jnp.sum(jnp.where(matches, pattern[None, :], 0), axis=1)


def per_device(
    ancestor_cov,
    ancestor_pattern,
    parent_panel,
    parent_inverse,
    child_pattern,
    child_panel,
    child_inverse,
):
    row_index = lax.axis_index("brow")
    column_index = lax.axis_index("bcol")
    row_devices = lax.axis_size("brow")
    local_rows = parent_panel.shape[0]
    band_rows = parent_inverse.shape[0]
    band_columns = parent_inverse.shape[1]
    ancestor_keep = block_keep(
        ancestor_pattern, row_index * local_rows, local_rows, local_rows * row_devices
    )
    child_keep = block_keep(
        child_pattern, row_index * band_rows, band_rows, band_rows * row_devices
    )
    parent_masked = parent_panel * ancestor_keep[:, None].astype(jnp.bfloat16)
    child_masked = child_panel * child_keep[:, None].astype(jnp.bfloat16)
    panel_slab = lax.dynamic_slice_in_dim(
        parent_masked, column_index * band_columns, band_columns, 1
    )
    parent_columns, child_columns = (
        lax.all_gather(panel_slab, "brow", axis=0, tiled=True),
        lax.all_gather(child_masked, "brow", axis=0, tiled=True),
    )
    factor_rows = parent_columns
    ancestor_sum = jnp.dot(
        lax.all_gather(ancestor_cov, "bcol", axis=1, tiled=True),
        factor_rows,
        preferred_element_type=jnp.float32,
    )
    ancestor_block = (-ancestor_sum * ancestor_keep[:, None].astype(jnp.float32)).astype(
        jnp.bfloat16
    )
    parent_wide = lax.all_to_all(parent_masked, "brow", split_axis=1, concat_axis=0, tiled=True)
    image_band = lax.all_gather(ancestor_block, "brow", axis=0, tiled=True)
    parent_inner = jnp.einsum(
        "ka,kb->ab", parent_wide, image_band, preferred_element_type=jnp.float32
    )
    parent_diag = (parent_inverse.astype(jnp.float32) - parent_inner).astype(jnp.bfloat16)
    factor_rows = child_columns
    parent_sum = jnp.dot(
        lax.all_gather(parent_diag, "bcol", axis=1, tiled=True),
        factor_rows,
        preferred_element_type=jnp.float32,
    )
    parent_child = (-parent_sum * child_keep[:, None].astype(jnp.float32)).astype(jnp.bfloat16)
    child_band = lax.all_gather(child_masked, "bcol", axis=1, tiled=True)
    child_inner = lax.psum_scatter(
        jnp.einsum("ka,kb->ab", child_band, parent_child, preferred_element_type=jnp.float32),
        "brow",
        scatter_dimension=0,
        tiled=True,
    )
    child_diag = (child_inverse.astype(jnp.float32) - child_inner).astype(jnp.bfloat16)
    return (ancestor_block, parent_diag, parent_child, child_diag)


def solution(mesh):
    return jax.shard_map(
        per_device,
        mesh=mesh,
        in_specs=(
            P("brow", "bcol"),
            P(),
            P("brow", None),
            P("brow", "bcol"),
            P(),
            P("brow", "bcol"),
            P("brow", "bcol"),
        ),
        out_specs=(P("brow", "bcol"), P("brow", "bcol"), P("brow", "bcol"), P("brow", "bcol")),
        check_vma=False,
    )
```

profile of v0, /device:TPU:8, one launch (start us, length us, event | category | flops | bytes accessed | tf_op | source)
XLA Modules:
  0.0 577.8 jit_solution(14311863399539205714)
XLA Ops:
  7.2 0.7 select_reduce_fusion
  8.0 2.1 broadcast_multiply_fusion
  10.1 0.7 constant_dynamic-slice_fusion
  10.8 0.7 all-gather.9.cloned.1.call-update
  11.5 1.9 copy.16
  13.4 15.2 %all-to-all-start = ((bf16[352,16,256]{2,0,1:T(8,128)(2,1)}), bf16[352,16,256]{2,0,1:T(8,128)(2,1)S(1)}, u32[]{:S(2)}, u32[]{:S(2)}) async-start(bf16[352,16,256]{2,0,1:T(8,128)(2,1)} %bitcast.19), calls=%async_computation | async-start | bytes 5767168 | tf_op jit(solution)/shard_map/all_to_all | solution.py:54
  28.6 0.0 all-gather.11.cloned.1.call-start
  28.7 119.7 %all-gather.7.cloned.1.call-done = bf16[5632,128]{1,0:T(8,128)(2,1)} async-done(((bf16[352,128]{1,0:T(8,128)(2,1)}), bf16[5632,128]{1,0:T(8,128)(2,1)}) %all-gather.7.cloned.1.call-update) | async-done | bytes 1441808 | tf_op jit(solution)/shard_map/all_gather | solution.py:42
  148.3 73.0 %all-gather.9.cloned.1.call-done = bf16[352,5632]{0,1:T(8,128)(2,1)} async-done(((bf16[352,176]{0,1:T(8,128)(2,1)}), bf16[352,5632]{0,1:T(8,128)(2,1)}) %all-gather.9.cloned.1.call-update) | async-done | bytes 3964944 | tf_op jit(solution)/shard_map/all_gather | solution.py:47
  221.3 5.1 fusion.5
  226.4 0.0 all-gather.15.cloned.1.call-start
  226.5 0.1 select_reduce_fusion.1
  226.6 0.7 broadcast_multiply_fusion.1
  227.4 0.0 all-gather.13.cloned.1.call-start
  227.4 71.0 %all-gather.11.cloned.1.call-done = bf16[5632,128]{1,0:T(8,128)(2,1)} async-done(((bf16[352,128]{1,0:T(8,128)(2,1)}), bf16[5632,128]{1,0:T(8,128)(2,1)}) %all-gather.11.cloned.1.call-update) | async-done | bytes 1441808 | tf_op jit(solution)/shard_map/all_gather | solution.py:55
  298.4 2.9 fusion.3
  301.4 0.5 all-gather.17.cloned.1.call-update
  302.0 66.9 %all-gather.15.cloned.1.call-done = bf16[4096,128]{1,0:T(8,128)(2,1)} async-done(((bf16[256,128]{1,0:T(8,128)(2,1)}), bf16[4096,128]{1,0:T(8,128)(2,1)}) %all-gather.15.cloned.1.call-update) | async-done | bytes 1048592 | tf_op jit(solution)/shard_map/all_gather | solution.py:43
  368.9 60.1 %all-gather.13.cloned.1.call-done = bf16[256,4096]{1,0:T(8,128)(2,1)} async-done(((bf16[256,128]{1,0:T(8,128)(2,1)}), bf16[256,4096]{1,0:T(8,128)(2,1)}) %all-gather.13.cloned.1.call-update) | async-done | bytes 2097168 | tf_op jit(solution)/shard_map/all_gather | solution.py:62
  429.0 2.6 fusion.4
  431.6 60.5 %all-gather.17.cloned.1.call-done = bf16[256,4096]{1,0:T(8,128)(2,1)} async-done(((bf16[256,128]{1,0:T(8,128)(2,1)}), bf16[256,4096]{1,0:T(8,128)(2,1)}) %all-gather.17.cloned.1.call-update) | async-done | bytes 2097168 | tf_op jit(solution)/shard_map/all_gather | solution.py:67
  492.2 3.7 fusion.11
  495.8 73.5 %reduce-scatter.2.cloned.1.call-done = f32[256,128]{1,0:T(8,128)} async-done(((f32[4096,128]{1,0:T(8,128)}), f32[256,128]{1,0:T(8,128)}) %reduce-scatter.2.cloned.1.call-update) | async-done | bytes 131088 | tf_op jit(solution)/shard_map/reduce_scatter | solution.py:68
  569.4 1.5 subtract_convert_fusion
  (24 shorter events, 0.3 us)
Async XLA Ops:
  7.2 141.2 %all-gather.7.cloned.1.call-start = ((), (), s32[]{:S(2)}) async-start(), calls=%async_computation.2 | async-start | bytes 1531904 | tf_op jit(solution)/shard_map/all_gather | solution.py:42
  10.8 210.5 %all-gather.9.cloned.1.call-start = ((), (), s32[]{:S(2)}) async-start(), calls=%async_computation.3 | async-start | bytes 4460544 | tf_op jit(solution)/shard_map/all_gather | solution.py:47
  13.4 285.0 %all-to-all-start = ((bf16[352,16,256]{2,0,1:T(8,128)(2,1)}), bf16[352,16,256]{2,0,1:T(8,128)(2,1)S(1)}, u32[]{:S(2)}, u32[]{:S(2)}) async-start(bf16[352,16,256]{2,0,1:T(8,128)(2,1)} %bitcast.19), calls=%async_computation | async-start | bytes 5767168 | tf_op jit(solution)/shard_map/all_to_all | solution.py:54
  28.6 269.8 %all-gather.11.cloned.1.call-start = ((), (), s32[]{:S(2)}) async-start(), calls=%async_computation.4 | async-start | bytes 1531904 | tf_op jit(solution)/shard_map/all_gather | solution.py:55
  221.3 5.2 copy-start.4
  221.3 5.3 copy-start.2
  221.3 77.1 %copy-start.1 = (bf16[256,128]{1,0:T(8,128)(2,1)S(1)}, bf16[256,128]{1,0:T(8,128)(2,1)}, u32[]{:S(2)}) copy-start(bf16[256,128]{1,0:T(8,128)(2,1)} %param.10) | copy-start | bytes 196612
  226.4 142.5 %all-gather.15.cloned.1.call-start = ((), (), s32[]{:S(2)}) async-start(), calls=%async_computation.6 | async-start | bytes 1114112 | tf_op jit(solution)/shard_map/all_gather | solution.py:43
  227.4 201.7 %all-gather.13.cloned.1.call-start = ((), (), s32[]{:S(2)}) async-start(), calls=%async_computation.5 | async-start | bytes 2162688 | tf_op jit(solution)/shard_map/all_gather | solution.py:62
  301.4 190.8 %all-gather.17.cloned.1.call-start = ((), (), s32[]{:S(2)}) async-start(), calls=%async_computation.7 | async-start | bytes 2162688 | tf_op jit(solution)/shard_map/all_gather | solution.py:67
  302.0 267.4 %reduce-scatter.2.cloned.1.call-start = ((), (), s32[]{:S(2)}) async-start(), calls=%async_computation.8 | async-start | bytes 2228224 | tf_op jit(solution)/shard_map/reduce_scatter | solution.py:68
  431.6 64.2 %copy-start = (bf16[256,128]{1,0:T(8,128)(2,1)}, bf16[256,128]{1,0:T(8,128)(2,1)S(1)}, u32[]{:S(2)}) copy-start(bf16[256,128]{1,0:T(8,128)(2,1)S(1)} %fusion.4) | copy-start | bytes 196612
  495.8 73.6 %copy-start.3 = (bf16[256,128]{1,0:T(8,128)(2,1)S(1)}, bf16[256,128]{1,0:T(8,128)(2,1)}, u32[]{:S(2)}) copy-start(bf16[256,128]{1,0:T(8,128)(2,1)} %param.13) | copy-start | bytes 196612
Sparse Core Ops, SparseCore 0:
  10.9 137.3 all-gather.6
  151.5 69.7 all-gather.8
  226.5 71.8 all-gather.10
  300.9 67.9 all-gather.14
  372.4 56.5 all-gather.12
  432.5 59.5 all-gather.16
  496.0 73.3 reduce-scatter.1
where the time goes:
time: 578 us
  waiting for transfers between devices  526 us (91%)
  starting transfers between devices  15.5 us (3%)
  matrix products  14.2 us (2%)
  between operations  14.2 us (2%)
    all_gather x1, waiting for transfers between devices, per_device(): lax.all_gather(panel_slab, 'brow', axis=0, tiled=True)  120 us
    reduce_scatter x1, waiting for transfers between devices, per_device(): lax.psum_scatter(jnp.einsum('ka,kb->ab', child_band, parent_child, prefer...  73.5 us
    all_gather x1, waiting for transfers between devices, per_device(): lax.all_gather(ancestor_cov, 'bcol', axis=1, tiled=True)  73 us
    all_gather x1, waiting for transfers between devices, per_device(): image_band = lax.all_gather(ancestor_block, 'brow', axis=0, tiled=True)  71 us
    all_gather x1, waiting for transfers between devices, per_device(): lax.all_gather(child_masked, 'brow', axis=0, tiled=True)  66.9 us
    all_gather x1, waiting for transfers between devices, per_device(): child_band = lax.all_gather(child_masked, 'bcol', axis=1, tiled=True)  60.5 us
    all_gather x1, waiting for transfers between devices, per_device(): lax.all_gather(parent_diag, 'bcol', axis=1, tiled=True)  60.1 us
    all_to_all x1, starting transfers between devices, per_device(): lax.all_to_all(parent_masked, 'brow', split_axis=1, concat_axis=0, tiled=...  15.2 us
  transfers between devices with their start and end apart: 8, of which 7 were waited for; matrix products, arithmetic and copies ran while one was open for 2% of the time, Pallas kernels for 0%

commit v1 on v0

--- a/solution.py
+++ b/solution.py
@@ -2,6 +2,18 @@
 import jax.numpy as jnp
 from jax import lax
 from jax.sharding import PartitionSpec as P
+
+
+def doubled_up(x, axis, dim):
+    ways, here = (lax.axis_size(axis), lax.axis_index(axis))
+    grown, reach = (x, 1)
+    while reach < ways:
+        theirs = lax.ppermute(grown, axis, [(d, d ^ reach) for d in range(ways)])
+        mine_first = jnp.concatenate([grown, theirs], axis=dim)
+        theirs_first = jnp.concatenate([theirs, grown], axis=dim)
+        grown = jnp.where(here & reach == 0, mine_first, theirs_first)
+        reach = 2 * reach
+    return grown
 
 
 def block_keep(pattern, first_row, count, total_rows):
@@ -64,7 +76,7 @@
         preferred_element_type=jnp.float32,
     )
     parent_child = (-parent_sum * child_keep[:, None].astype(jnp.float32)).astype(jnp.bfloat16)
-    child_band = lax.all_gather(child_masked, "bcol", axis=1, tiled=True)
+    child_band = doubled_up(child_masked, "bcol", 1)
     child_inner = lax.psum_scatter(
         jnp.einsum("ka,kb->ab", child_band, parent_child, preferred_element_type=jnp.float32),
         "brow",

time: 578 us -> 517 us (0.89)
  the two profiles are of different devices: /device:TPU:8 before, /device:TPU:10 now
where the time goes in v1:
time: 517 us
  waiting for transfers between devices  451 us (87%)
  starting transfers between devices  30.3 us (6%)
  between operations  14.3 us (3%)
  matrix products  12.7 us (2%)
  other arithmetic  5.87 us (1%)
    all_gather x1, waiting for transfers between devices, per_device(): lax.all_gather(panel_slab, 'brow', axis=0, tiled=True)  126 us
    reduce_scatter x1, waiting for transfers between devices, per_device(): lax.psum_scatter(jnp.einsum('ka,kb->ab', child_band, parent_child, prefer...  74.7 us
    all_gather x1, waiting for transfers between devices, per_device(): image_band = lax.all_gather(ancestor_block, 'brow', axis=0, tiled=True)  72.2 us
    all_gather x1, waiting for transfers between devices, per_device(): lax.all_gather(ancestor_cov, 'bcol', axis=1, tiled=True)  66 us
    all_gather x1, waiting for transfers between devices, per_device(): lax.all_gather(parent_diag, 'bcol', axis=1, tiled=True)  59 us
    all_gather x1, waiting for transfers between devices, per_device(): lax.all_gather(child_masked, 'brow', axis=0, tiled=True)  27.1 us
    ppermute x5, waiting for transfers between devices, doubled_up(): theirs = lax.ppermute(grown, axis, [(d, d ^ reach) for d in range(ways)])  24.8 us
    all_to_all x1, starting transfers between devices, per_device(): lax.all_to_all(parent_masked, 'brow', split_axis=1, concat_axis=0, tiled=...  15.2 us
  transfers between devices with their start and end apart: 12, of which 10 were waited for; matrix products, arithmetic and copies ran while one was open for 3% of the time, Pallas kernels for 0%

profile of v1, /device:TPU:10, one launch (start us, length us, event | category | flops | bytes accessed | tf_op | source)
XLA Modules:
  0.0 516.9 jit_solution(11266178631856862601)
XLA Ops:
  7.2 0.7 select_reduce_fusion
  8.0 2.1 broadcast_multiply_fusion
  11.5 1.9 copy.16
  13.4 15.2 %all-to-all-start = ((bf16[352,16,256]{2,0,1:T(8,128)(2,1)}), bf16[352,16,256]{2,0,1:T(8,128)(2,1)S(1)}, u32[]{:S(2)}, u32[]{:S(2)}) async-start(bf16[352,16,256]{2,0,1:T(8,128)(2,1)} %bitcast.18), calls=%async_computation | async-start | bytes 5767168 | tf_op jit(solution)/shard_map/all_to_all | solution.py:66
  28.7 126.5 %all-gather.6.cloned.1.call-done = bf16[5632,128]{1,0:T(8,128)(2,1)} async-done(((bf16[352,128]{1,0:T(8,128)(2,1)}), bf16[5632,128]{1,0:T(8,128)(2,1)}) %all-gather.6.cloned.1.call-update) | async-done | bytes 1441808 | tf_op jit(solution)/shard_map/all_gather | solution.py:54
  155.2 66.0 %all-gather.8.cloned.1.call-done = bf16[352,5632]{0,1:T(8,128)(2,1)} async-done(((bf16[352,176]{0,1:T(8,128)(2,1)}), bf16[352,5632]{0,1:T(8,128)(2,1)}) %all-gather.8.cloned.1.call-update) | async-done | bytes 3964944 | tf_op jit(solution)/shard_map/all_gather | solution.py:59
  221.1 5.1 fusion.12
  227.2 72.2 %all-gather.10.cloned.1.call-done = bf16[5632,128]{1,0:T(8,128)(2,1)} async-done(((bf16[352,128]{1,0:T(8,128)(2,1)}), bf16[5632,128]{1,0:T(8,128)(2,1)}) %all-gather.10.cloned.1.call-update) | async-done | bytes 1441808 | tf_op jit(solution)/shard_map/all_gather | solution.py:67
  299.5 3.0 fusion.10
  302.5 1.9 collective-permute-start
  304.5 1.2 collective-permute-done
  305.7 2.5 collective-permute-start.1
  308.2 5.0 collective-permute-done.1
  313.3 4.0 collective-permute-start.2
  317.3 6.9 %collective-permute-done.2 = bf16[256,512]{1,0:T(8,128)(2,1)S(1)} collective-permute-done((bf16[256,512]{1,0:T(8,128)(2,1)S(1)}, bf16[256,512]{1,0:T(8,128)(2,1)S(1)}, u32[]{:S(2)}, u32[]{:S(2)}) %collective-permute-start.2) | collective-permute-done | bytes 262176 | tf_op jit(solution)/shard_map/ppermute | solution.py:11
  324.4 2.4 collective-permute-start.3
  326.8 11.7 %collective-permute-done.3 = bf16[256,1024]{1,0:T(8,128)(2,1)S(1)} collective-permute-done((bf16[256,1024]{1,0:T(8,128)(2,1)S(1)}, bf16[256,1024]{1,0:T(8,128)(2,1)S(1)}, u32[]{:S(2)}, u32[]{:S(2)}) %collective-permute-start.3) | collective-permute-done | bytes 524320 | tf_op jit(solution)/shard_map/ppermute | solution.py:11
  338.9 4.0 collective-permute-start.4
  342.9 27.1 %all-gather.14.cloned.1.call-done = bf16[4096,128]{1,0:T(8,128)(2,1)} async-done(((bf16[256,128]{1,0:T(8,128)(2,1)}), bf16[4096,128]{1,0:T(8,128)(2,1)}) %all-gather.14.cloned.1.call-update) | async-done | bytes 1048592 | tf_op jit(solution)/shard_map/all_gather | solution.py:55
  370.0 59.0 %all-gather.12.cloned.1.call-done = bf16[256,4096]{1,0:T(8,128)(2,1)} async-done(((bf16[256,128]{1,0:T(8,128)(2,1)}), bf16[256,4096]{1,0:T(8,128)(2,1)}) %all-gather.12.cloned.1.call-update) | async-done | bytes 2097168 | tf_op jit(solution)/shard_map/all_gather | solution.py:74
  429.0 2.6 fusion.11
  431.6 2.1 fusion
  433.7 74.7 %reduce-scatter.2.cloned.1.call-done = f32[256,128]{1,0:T(8,128)} async-done(((f32[4096,128]{1,0:T(8,128)}), f32[256,128]{1,0:T(8,128)}) %reduce-scatter.2.cloned.1.call-update) | async-done | bytes 131088 | tf_op jit(solution)/shard_map/reduce_scatter | solution.py:80
  508.5 1.5 subtract_convert_fusion
  (37 shorter events, 3.2 us)
Async XLA Ops:
  7.2 148.0 %all-gather.6.cloned.1.call-start = ((), (), s32[]{:S(2)}) async-start(), calls=%async_computation.2 | async-start | bytes 1531904 | tf_op jit(solution)/shard_map/all_gather | solution.py:54
  10.8 210.4 %all-gather.8.cloned.1.call-start = ((), (), s32[]{:S(2)}) async-start(), calls=%async_computation.3 | async-start | bytes 4460544 | tf_op jit(solution)/shard_map/all_gather | solution.py:59
  13.4 286.0 %all-to-all-start = ((bf16[352,16,256]{2,0,1:T(8,128)(2,1)}), bf16[352,16,256]{2,0,1:T(8,128)(2,1)S(1)}, u32[]{:S(2)}, u32[]{:S(2)}) async-start(bf16[352,16,256]{2,0,1:T(8,128)(2,1)} %bitcast.18), calls=%async_computation | async-start | bytes 5767168 | tf_op jit(solution)/shard_map/all_to_all | solution.py:66
  28.6 270.8 %all-gather.10.cloned.1.call-start = ((), (), s32[]{:S(2)}) async-start(), calls=%async_computation.4 | async-start | bytes 1531904 | tf_op jit(solution)/shard_map/all_gather | solution.py:67
  221.1 5.2 %copy-start.5 = (s32[16]{0:T(128)S(1)}, s32[16]{0:T(128)}, u32[]{:S(2)}) copy-start(s32[16]{0:T(128)} %param.11) | copy-start | bytes 196
  221.1 5.3 %copy-start.3 = (bf16[256,128]{1,0:T(8,128)(2,1)S(1)}, bf16[256,128]{1,0:T(8,128)(2,1)}, u32[]{:S(2)}) copy-start(bf16[256,128]{1,0:T(8,128)(2,1)} %param.12) | copy-start | bytes 196612
  221.1 78.3 %copy-start.1 = (bf16[256,128]{1,0:T(8,128)(2,1)S(1)}, bf16[256,128]{1,0:T(8,128)(2,1)}, u32[]{:S(2)}) copy-start(bf16[256,128]{1,0:T(8,128)(2,1)} %param.10) | copy-start | bytes 196612
  226.2 143.8 %all-gather.14.cloned.1.call-start = ((), (), s32[]{:S(2)}) async-start(), calls=%async_computation.6 | async-start | bytes 1114112 | tf_op jit(solution)/shard_map/all_gather | solution.py:55
  227.2 201.8 %all-gather.12.cloned.1.call-start = ((), (), s32[]{:S(2)}) async-start(), calls=%async_computation.5 | async-start | bytes 2162688 | tf_op jit(solution)/shard_map/all_gather | solution.py:74
  299.5 3.1 copy-start
  302.5 206.0 %reduce-scatter.2.cloned.1.call-start = ((), (), s32[]{:S(2)}) async-start(), calls=%async_computation.7 | async-start | bytes 2228224 | tf_op jit(solution)/shard_map/reduce_scatter | solution.py:80
  302.5 3.1 collective-permute-start
  305.7 7.5 %collective-permute-start.1 = (bf16[256,256]{1,0:T(8,128)(2,1)S(1)}, bf16[256,256]{1,0:T(8,128)(2,1)S(1)}, u32[]{:S(2)}, u32[]{:S(2)}) collective-permute-start(bf16[256,256]{1,0:T(8,128)(2,1)S(1)} %maximum_select_fusion.5), channel_id=1, source_target_pairs={{0,2},{1,3},{2,0},{3,1},{4,6},{5,7},{6,4},{7,5},{8,10},{9,11},{10,... | collective-permute-start | bytes 393224 | tf_op jit(solution)/shard_map/ppermute | solution.py:11
  313.3 10.9 %collective-permute-start.2 = (bf16[256,512]{1,0:T(8,128)(2,1)S(1)}, bf16[256,512]{1,0:T(8,128)(2,1)S(1)}, u32[]{:S(2)}, u32[]{:S(2)}) collective-permute-start(bf16[256,512]{1,0:T(8,128)(2,1)S(1)} %maximum_select_fusion.4), channel_id=1, source_target_pairs={{0,4},{1,5},{2,6},{3,7},{4,0},{5,1},{6,2},{7,3},{8,12},{9,13},{10,... | collective-permute-start | bytes 786440 | tf_op jit(solution)/shard_map/ppermute | solution.py:11
  324.4 14.1 %collective-permute-start.3 = (bf16[256,1024]{1,0:T(8,128)(2,1)S(1)}, bf16[256,1024]{1,0:T(8,128)(2,1)S(1)}, u32[]{:S(2)}, u32[]{:S(2)}) collective-permute-start(bf16[256,1024]{1,0:T(8,128)(2,1)S(1)} %maximum_select_fusion.3), channel_id=1, source_target_pairs={{0,8},{1,9},{2,10},{3,11},{4,12},{5,13},{6,14},{7,15},{8,0},{9,1},... | collective-permute-start | bytes 1572872 | tf_op jit(solution)/shard_map/ppermute | solution.py:11
  338.9 92.7 %collective-permute-start.4 = (bf16[256,2048]{1,0:T(8,128)(2,1)S(1)}, bf16[256,2048]{1,0:T(8,128)(2,1)S(1)}, u32[]{:S(2)}, u32[]{:S(2)}) collective-permute-start(bf16[256,2048]{1,0:T(8,128)(2,1)S(1)} %maximum_select_fusion.2), channel_id=1, source_target_pairs={{0,16},{1,17},{2,18},{3,19},{4,20},{5,21},{6,22},{7,23},{8,24},{9,... | collective-permute-start | bytes 3145736 | tf_op jit(solution)/shard_map/ppermute | solution.py:11
  431.6 2.1 copy-start.2
  433.7 74.8 %copy-start.4 = (bf16[256,128]{1,0:T(8,128)(2,1)S(1)}, bf16[256,128]{1,0:T(8,128)(2,1)}, u32[]{:S(2)}) copy-start(bf16[256,128]{1,0:T(8,128)(2,1)} %param.13) | copy-start | bytes 196612
Sparse Core Ops, SparseCore 0:
  10.9 144.2 all-gather.5
  158.3 62.7 all-gather.7
  226.4 73.0 all-gather.9
  302.0 68.0 all-gather.13
  373.5 55.4 all-gather.11
  433.8 74.5 reduce-scatter.1
